TPU v7x, 512 devices: a whole 4x8x8 slice. The times are simulated.
512 devices in a mesh: group: 8 (over y_lo, x), tp: 64 (over z, y_hi, core).
Axes of the slice: x: 4, y: 8 (y_hi: 4, y_lo: 2; y = y_hi * 2 + y_lo), z: 8, core: 2. Of those that a mesh axis runs over, the one named last changes fastest.
Arguments:
- hidden: bfloat16 [1024, 12288], P('group', 'tp')
- q_weight: bfloat16 [12288, 12288], P('group', 'tp'), may hold values from -0.0546875 to 0.0546875
- kv_weight: bfloat16 [12288, 2048], P('group', 'tp'), may hold values from -0.0546875 to 0.0546875
- o_weight: bfloat16 [12288, 12288], P('group', 'tp'), may hold values from -0.3125 to 0.3125
- k_pool: bfloat16 [12288, 32, 1024], P(('group', 'tp'))
- v_pool: bfloat16 [12288, 32, 1024], P(('group', 'tp')), may hold values from -6 to 6
- page_table: int32 [1024, 12], P(('group', 'tp')), may hold values from 0 to 23, as said below
- lengths: int32 [1024], P(('group', 'tp')), may hold values from 1 to 384, as said below
Outputs:
- attended: bfloat16 [1024, 12288], P('group', 'tp')
- new_kv: bfloat16 [1024, 2048], P(('group', 'tp'))
Inputs may be any that keep to these rules, and one draw needn't show every extreme that they name: `page_table`: the 2 requests of each aligned block name each of that device's 24 page slots exactly once. `lengths`: the first request of each aligned block of 2 requests has exactly 384 cached tokens.
All inputs are finite; a program needn't handle non-finite values.
Results may differ from a plain program's by a relative error of at most 0.01.
Values may be sent and summed in bfloat16 or wider, within the bound.
No kernel may reach another device: no remote copies, remote signals or barrier semaphores. Data moves between devices by JAX's collectives and lax.ppermute only.
A program may use at most 64 MiB of HBM per device.

v0:
```python
import jax
import jax.numpy as jnp
from jax import lax
from jax.sharding import PartitionSpec as P

D = 12288
HD = 128
eps = 1e-05


def attend_rows(q_rows, kv_rows, k_pool, v_pool, page_table, lengths):
    nrows = q_rows.shape[0]
    kv_width = k_pool.shape[2]
    kv_heads = kv_width // HD
    per_group = q_rows.shape[1] // HD // kv_heads
    query = q_rows.reshape(nrows, kv_heads, per_group, HD)
    own_keys = kv_rows[:, :kv_width].reshape(nrows, kv_heads, HD)
    own_values = kv_rows[:, kv_width:].reshape(nrows, kv_heads, HD)
    paged_keys = k_pool[page_table].reshape(nrows, -1, kv_heads, HD)
    paged_values = v_pool[page_table].reshape(nrows, -1, kv_heads, HD)
    scale = 1.0 / jnp.sqrt(jnp.float32(HD))
    cached = (
        jnp.einsum("rgph,rcgh->rgpc", query, paged_keys, preferred_element_type=jnp.float32) * scale
    )
    own = jnp.einsum("rgph,rgh->rgp", query, own_keys, preferred_element_type=jnp.float32) * scale
    context = paged_keys.shape[1]
    valid = jnp.arange(context, dtype=jnp.int32)[None, :] < lengths[:, None]
    cached = jnp.where(valid[:, None, None, :], cached, jnp.float32(-1e30))
    top = jnp.maximum(jnp.max(cached, axis=-1), own)
    exp_cached = jnp.exp(cached - top[..., None])
    exp_own = jnp.exp(own - top)
    total = jnp.sum(exp_cached, axis=-1) + exp_own
    weight_cached = (exp_cached / total[..., None]).astype(jnp.bfloat16)
    weight_own = (exp_own / total).astype(jnp.bfloat16)
    mixed = jnp.einsum(
        "rgpc,rcgh->rgph", weight_cached, paged_values, preferred_element_type=jnp.float32
    )
    mixed = mixed + weight_own[..., None].astype(jnp.float32) * own_values[:, :, None, :].astype(
        jnp.float32
    )
    return mixed.astype(jnp.bfloat16).reshape(nrows, -1)


def per_device(hidden, q_weight, kv_weight, o_weight, k_pool, v_pool, page_table, lengths):
    q_whole, kv_whole = (
        lax.all_gather(q_weight, "group", axis=0, tiled=True),
        lax.all_gather(kv_weight, "group", axis=0, tiled=True),
    )
    o_whole = lax.all_gather(o_weight, "group", axis=0, tiled=True)
    piece = lax.all_gather(hidden, "tp", axis=1, tiled=True)
    widened = piece.astype(jnp.float32)
    q_total = jnp.dot(piece, q_whole, preferred_element_type=jnp.float32)
    kv_total = jnp.dot(piece, kv_whole, preferred_element_type=jnp.float32)
    squares = jnp.sum(widened * widened, axis=1)
    inv_rms = lax.rsqrt(squares / D + eps)[:, None]
    queries = (q_total * inv_rms).astype(jnp.bfloat16)
    fresh = (kv_total * inv_rms).astype(jnp.bfloat16)
    q_rows, kv_rows = (
        lax.all_to_all(queries, "tp", split_axis=0, concat_axis=1, tiled=True),
        lax.all_to_all(fresh, "tp", split_axis=0, concat_axis=1, tiled=True),
    )
    mixed = attend_rows(q_rows, kv_rows, k_pool, v_pool, page_table, lengths)
    by_columns = lax.all_to_all(mixed, "tp", split_axis=1, concat_axis=0, tiled=True)
    attended = jnp.dot(
        lax.all_gather(by_columns, "tp", axis=1, tiled=True),
        o_whole,
        preferred_element_type=jnp.float32,
    )
    return (attended.astype(jnp.bfloat16), kv_rows)


def solution(mesh):
    in_specs = (
        P("group", "tp"),
        P("group", "tp"),
        P("group", "tp"),
        P("group", "tp"),
        P(("group", "tp"), None, None),
        P(("group", "tp"), None, None),
        P(("group", "tp"), None),
        P(("group", "tp")),
    )
    out_specs = (P("group", "tp"), P(("group", "tp"), None))
    return jax.shard_map(
        per_device, mesh=mesh, in_specs=in_specs, out_specs=out_specs, check_vma=False
    )
```

profile of v0, /device:TPU:1, one launch (start us, length us, event | category | flops | bytes accessed | tf_op | source)
XLA Modules:
  0.0 330.4 jit_solution(7475533996092343099)
XLA Ops:
  7.2 0.0 copy-start
  7.2 0.0 all-gather.5.cloned.1.call-start
  7.2 0.7 all-gather.5.cloned.1.call-update
  7.9 0.0 all-gather.7.cloned.1.call-start
  8.0 0.7 all-gather.7.cloned.1.call-update
  8.7 0.0 all-gather.11.cloned.1.call-start
  8.7 0.7 all-gather.11.cloned.1.call-update
  9.4 0.7 compare_select_fusion
  10.1 0.1 reshape.70
  10.2 0.7 iota_compare_fusion
  10.9 24.9 %all_gather.17 = bf16[12288,32]{0,1:T(8,128)(2,1)S(1)} all-gather(bf16[1536,32]{0,1:T(8,128)(2,1)} %param.10), channel_id=1, replica_groups=mesh['group'=8,'tp'=64] {'group'}, dimensions={0}, use_global_device_ids=true | all-gather | bytes 884736 | tf_op jit(solution)/shard_map/all_gather | solution.py:47
  35.8 67.1 %all-gather.5.cloned.1.call-done = bf16[128,12288]{0,1:T(8,128)(2,1)} async-done(((bf16[128,192]{0,1:T(8,128)(2,1)}), bf16[128,12288]{0,1:T(8,128)(2,1)}) %all-gather.5.cloned.1.call-update) | async-done | bytes 3145744 | tf_op jit(solution)/shard_map/all_gather | solution.py:50
  102.9 0.0 copy-start.1
  102.9 3.2 multiply_reduce_fusion
  106.1 0.0 copy-done.1
  106.1 0.6 fusion.17
  106.7 0.7 copy.24
  107.5 7.1 %all-to-all-start.1 = ((bf16[64,2,32]{2,1,0:T(2,128)(2,1)}), bf16[64,2,32]{2,1,0:T(2,128)(2,1)S(1)}, u32[]{:S(2)}, u32[]{:S(2)}) async-start(bf16[64,2,32]{2,1,0:T(2,128)(2,1)} %bitcast.1), calls=%async_computation.1 | async-start | bytes 65536 | tf_op jit(solution)/shard_map/all_to_all | solution.py:60
  114.6 0.0 copy-done
  114.6 1.9 gather_fusion
  116.5 1.8 copy.31
  118.3 3.3 gather_fusion.1
  121.6 3.1 copy.32
  124.6 1.6 all-to-all-done.1
  126.3 0.1 all_to_all.46
  126.4 0.0 copy-start.2
  126.4 38.2 %all-gather.7.cloned.1.call-done = bf16[12288,192]{0,1:T(8,128)(2,1)} async-done(((bf16[1536,192]{0,1:T(8,128)(2,1)}), bf16[12288,192]{0,1:T(8,128)(2,1)}) %all-gather.7.cloned.1.call-update) | async-done | bytes 4718608 | tf_op jit(solution)/shard_map/all_gather | solution.py:46
  164.6 4.7 %fusion.16 = bf16[128,192]{0,1:T(8,128)(2,1)S(1)} fusion(bf16[12288,192]{0,1:T(8,128)(2,1)} %all-gather.7.cloned.1.call-done, bf16[128,12288]{0,1:T(8,128)(2,1)} %all-gather.5.cloned.1.call-done, f32[128]{0:T(128)S(1)} %add_rsqrt_fusion), kind=kOutput, calls=%fused_computation.12 | convolution fusion | flops 604028928 | bytes 7913984 | tf_op jit(solution)/shard_map/dot_general | solution.py:52
  169.3 0.1 copy.21
  169.5 0.7 all_to_all.40
  170.1 12.4 %all-to-all-start = ((bf16[64,2,192]{2,1,0:T(2,128)(2,1)}), bf16[64,2,192]{2,1,0:T(2,128)(2,1)S(1)}, u32[]{:S(2)}, u32[]{:S(2)}) async-start(bf16[64,2,192]{2,1,0:T(2,128)(2,1)} %all_to_all.40), calls=%async_computation | async-start | bytes 131072 | tf_op jit(solution)/shard_map/all_to_all | solution.py:59
  182.6 0.0 all-gather.9.cloned.1.call-start
  182.6 0.0 copy-done.2
  182.7 13.0 %all-to-all-done = bf16[64,2,192]{2,1,0:T(2,128)(2,1)S(1)} async-done(((bf16[64,2,192]{2,1,0:T(2,128)(2,1)}), bf16[64,2,192]{2,1,0:T(2,128)(2,1)S(1)}, u32[]{:S(2)}, u32[]{:S(2)}) %all-to-all-start) | async-done | bytes 49184 | tf_op jit(solution)/shard_map/all_to_all | solution.py:59
  195.6 0.1 reshape.63
  195.8 0.1 fusion.24
  195.9 0.7 fusion.23
  196.6 0.2 fusion.18
  196.9 1.9 fusion.13
  198.8 0.1 all_to_all.47
  198.9 0.1 copy.27
  199.0 16.9 %all_to_all.54 = bf16[2,64,192]{2,0,1:T(2,128)(2,1)S(1)} all-to-all(bf16[2,64,192]{2,0,1:T(2,128)(2,1)S(1)} %copy.27), channel_id=1, replica_groups=mesh['group'=8,'tp'=64] {'tp'}, dimensions={1} | all-to-all | bytes 98304 | tf_op jit(solution)/shard_map/all_to_all | solution.py:63
  215.9 0.1 all_to_all.50
  215.9 0.7 copy.28
  216.7 0.0 all-gather.9.cloned.1.call-update
  216.7 13.9 %all-gather.11.cloned.1.call-done = bf16[12288,192]{0,1:T(8,128)(2,1)} async-done(((bf16[1536,192]{0,1:T(8,128)(2,1)}), bf16[12288,192]{0,1:T(8,128)(2,1)}) %all-gather.11.cloned.1.call-update) | async-done | bytes 4718608 | tf_op jit(solution)/shard_map/all_gather | solution.py:49
  230.5 88.0 %all-gather.9.cloned.1.call-done = bf16[128,12288]{0,1:T(8,128)(2,1)} async-done(((bf16[128,192]{0,1:T(8,128)(2,1)}), bf16[128,12288]{0,1:T(8,128)(2,1)}) %all-gather.9.cloned.1.call-update) | async-done | bytes 3145744 | tf_op jit(solution)/shard_map/all_gather | solution.py:65
  318.5 5.3 %convolution_convert_fusion = bf16[128,192]{0,1:T(8,128)(2,1)} fusion(bf16[12288,192]{0,1:T(8,128)(2,1)} %all-gather.11.cloned.1.call-done, bf16[128,12288]{0,1:T(8,128)(2,1)} %all-gather.9.cloned.1.call-done), kind=kOutput, calls=%fused_computation.13 | convolution fusion | flops 604004352 | bytes 7913472 | tf_op jit(solution)/shard_map/dot_general | solution.py:64
  (9 shorter events, 0.1 us)
Async XLA Ops:
  7.2 107.4 %copy-start = (bf16[24,32,1024]{2,1,0:T(8,128)(2,1)S(1)}, bf16[24,32,1024]{2,1,0:T(8,128)(2,1)}, u32[]{:S(2)}) copy-start(bf16[24,32,1024]{2,1,0:T(8,128)(2,1)} %param.12) | copy-start | bytes 4718596
  7.2 95.7 %all-gather.5.cloned.1.call-start = ((), (), s32[]{:S(2)}) async-start(), calls=%async_computation.3 | async-start | bytes 3194880 | tf_op jit(solution)/shard_map/all_gather | solution.py:50
  7.9 156.7 %all-gather.7.cloned.1.call-start = ((), (), s32[]{:S(2)}) async-start(), calls=%async_computation.4 | async-start | bytes 5308416 | tf_op jit(solution)/shard_map/all_gather | solution.py:46
  8.7 221.9 %all-gather.11.cloned.1.call-start = ((), (), s32[]{:S(2)}) async-start(), calls=%async_computation.6 | async-start | bytes 5308416 | tf_op jit(solution)/shard_map/all_gather | solution.py:49
  102.9 3.2 copy-start.1
  107.5 18.8 %all-to-all-start.1 = ((bf16[64,2,32]{2,1,0:T(2,128)(2,1)}), bf16[64,2,32]{2,1,0:T(2,128)(2,1)S(1)}, u32[]{:S(2)}, u32[]{:S(2)}) async-start(bf16[64,2,32]{2,1,0:T(2,128)(2,1)} %bitcast.1), calls=%async_computation.1 | async-start | bytes 65536 | tf_op jit(solution)/shard_map/all_to_all | solution.py:60
  126.4 56.2 %copy-start.2 = (bf16[2,2048]{1,0:T(2,128)(2,1)}, bf16[2,2048]{1,0:T(2,128)(2,1)S(1)}, u32[]{:S(2)}) copy-start(bf16[2,2048]{1,0:T(2,128)(2,1)S(1)} %all_to_all.46) | copy-start | bytes 24580
  170.1 25.5 %all-to-all-start = ((bf16[64,2,192]{2,1,0:T(2,128)(2,1)}), bf16[64,2,192]{2,1,0:T(2,128)(2,1)S(1)}, u32[]{:S(2)}, u32[]{:S(2)}) async-start(bf16[64,2,192]{2,1,0:T(2,128)(2,1)} %all_to_all.40), calls=%async_computation | async-start | bytes 131072 | tf_op jit(solution)/shard_map/all_to_all | solution.py:59
  182.6 135.9 %all-gather.9.cloned.1.call-start = ((), (), s32[]{:S(2)}) async-start(), calls=%async_computation.5 | async-start | bytes 3194880 | tf_op jit(solution)/shard_map/all_gather | solution.py:65
Sparse Core Ops, SparseCore 0:
  11.4 91.5 all-gather.4
  105.0 59.5 all-gather.6
  166.7 63.7 all-gather.10
  234.3 84.1 all-gather.8
where the time goes:
time: 331 us; the launch traced here: 330 us
  waiting for transfers between devices  224 us (68%)
  blocking collectives  41.8 us (13%)
  starting transfers between devices  19.7 us (6%)
  between operations  13.9 us (4%)
  matrix products  13.4 us (4%)
  local copies, waits for them, and re-layouts  12.9 us (4%)
  other arithmetic  4.89 us (1%)
    all_gather x1, waiting for transfers between devices, per_device(): lax.all_gather(by_columns, 'tp', axis=1, tiled=True)  88 us
    all_gather x1, waiting for transfers between devices, per_device(): piece = lax.all_gather(hidden, 'tp', axis=1, tiled=True)  67.1 us
    all_gather x1, waiting for transfers between devices, per_device(): lax.all_gather(q_weight, 'group', axis=0, tiled=True)  38.2 us
    all_gather x1, blocking collectives, per_device(): lax.all_gather(kv_weight, 'group', axis=0, tiled=True)  24.9 us
    all_to_all x1, blocking collectives, per_device(): lax.all_to_all(mixed, 'tp', split_axis=1, concat_axis=0, tiled=True)  16.9 us
    all_gather x1, waiting for transfers between devices, per_device(): o_whole = lax.all_gather(o_weight, 'group', axis=0, tiled=True)  13.9 us
    all_to_all x1, waiting for transfers between devices, per_device(): lax.all_to_all(queries, 'tp', split_axis=0, concat_axis=1, tiled=True)  13 us
    all_to_all x1, starting transfers between devices, per_device(): lax.all_to_all(queries, 'tp', split_axis=0, concat_axis=1, tiled=True)  12.4 us
  transfers between devices with their start and end apart: 6, of which 6 were waited for; matrix products, arithmetic and copies ran while one was open for 8% of the time, Pallas kernels for 0%

commit v1 on v0

--- a/solution.py
+++ b/solution.py
@@ -44,7 +44,9 @@
 def per_device(hidden, q_weight, kv_weight, o_weight, k_pool, v_pool, page_table, lengths):
     q_whole, kv_whole = (
         lax.all_gather(q_weight, "group", axis=0, tiled=True),
-        lax.all_gather(kv_weight, "group", axis=0, tiled=True),
+        jnp.concatenate(
+            lax.all_to_all(jnp.stack([kv_weight] * lax.axis_size("group")), "group", 0, 0), axis=0
+        ),
     )
     o_whole = lax.all_gather(o_weight, "group", axis=0, tiled=True)
     piece = lax.all_gather(hidden, "tp", axis=1, tiled=True)

time: 331 us -> 331 us (level)
  blocking collectives: 41.8 us -> 16.9 us
  waiting for transfers between devices: 224 us -> 242 us
  starting transfers between devices: 19.7 us -> 25.5 us
    all_gather x1 -> x0, blocking collectives: 24.9 us -> none  [per_device(): lax.all_gather(kv_weight, 'group', axis=0, tiled=True)]
    all_gather x1, waiting for transfers between devices: 67.1 us -> 77.3 us  [per_device(): piece = lax.all_gather(hidden, 'tp', axis=1, tiled=True)]
    all_to_all x0 -> x1, waiting for transfers between devices: none -> 8.16 us  [per_device(): lax.all_to_all(jnp.stack([kv_weight] * lax.axis_size('group')), 'group',...]
    all_to_all x0 -> x1, starting transfers between devices: none -> 5.88 us  [per_device(): lax.all_to_all(jnp.stack([kv_weight] * lax.axis_size('group')), 'group',...]
  transfers between devices with their start and end apart: 6 -> 7, of which waited for: 6 -> 7; matrix products, arithmetic and copies ran while one was open for 8% -> 8% of each run, Pallas kernels for 0% -> 0%
where the time goes in v1:
time: 331 us; the launch traced here: 330 us
  waiting for transfers between devices  242 us (73%)
  starting transfers between devices  25.5 us (8%)
  blocking collectives  16.9 us (5%)
  local copies, waits for them, and re-layouts  14.9 us (5%)
  between operations  14 us (4%)
  matrix products  13.4 us (4%)
  other arithmetic  3.55 us (1%)
    all_gather x1, waiting for transfers between devices, per_device(): lax.all_gather(by_columns, 'tp', axis=1, tiled=True)  88 us
    all_gather x1, waiting for transfers between devices, per_device(): piece = lax.all_gather(hidden, 'tp', axis=1, tiled=True)  77.3 us
    all_gather x1, waiting for transfers between devices, per_device(): lax.all_gather(q_weight, 'group', axis=0, tiled=True)  38.2 us
    all_to_all x1, blocking collectives, per_device(): lax.all_to_all(mixed, 'tp', split_axis=1, concat_axis=0, tiled=True)  16.9 us
    all_gather x1, waiting for transfers between devices, per_device(): o_whole = lax.all_gather(o_weight, 'group', axis=0, tiled=True)  13.9 us
    all_to_all x1, waiting for transfers between devices, per_device(): lax.all_to_all(queries, 'tp', split_axis=0, concat_axis=1, tiled=True)  13 us
    all_to_all x1, starting transfers between devices, per_device(): lax.all_to_all(queries, 'tp', split_axis=0, concat_axis=1, tiled=True)  12.4 us
    all_to_all x1, waiting for transfers between devices, per_device(): lax.all_to_all(jnp.stack([kv_weight] * lax.axis_size('group')), 'group',...  8.16 us
  transfers between devices with their start and end apart: 7, of which 7 were waited for; matrix products, arithmetic and copies ran while one was open for 8% of the time, Pallas kernels for 0%

profile of v1, /device:TPU:1, one launch (start us, length us, event | category | flops | bytes accessed | tf_op | source)
XLA Modules:
  0.0 330.4 jit_solution(13472899793438118511)
XLA Ops:
  7.2 0.0 copy-start
  7.2 0.0 copy-start.3
  7.2 0.0 all-gather.5.cloned.1.call-start
  7.2 0.7 all-gather.5.cloned.1.call-update
  7.9 0.0 all-gather.7.cloned.1.call-start
  8.0 0.7 all-gather.7.cloned.1.call-update
  8.7 0.0 all-gather.11.cloned.1.call-start
  8.7 0.7 all-gather.11.cloned.1.call-update
  9.4 1.9 stack.2
  11.3 5.9 %all-to-all-start.1 = ((bf16[8,1536,32]{1,2,0:T(8,128)(2,1)}), bf16[8,1536,32]{1,2,0:T(8,128)(2,1)S(1)}, u32[]{:S(2)}, u32[]{:S(2)}) async-start(bf16[8,1536,32]{1,2,0:T(8,128)(2,1)} %stack.2), calls=%async_computation.1 | async-start | bytes 1572864 | tf_op jit(solution)/shard_map/all_to_all | solution.py:48
  17.2 0.1 reshape.76
  17.3 0.1 iota_compare_fusion
  17.4 8.2 %all-to-all-done.1 = bf16[8,1536,32]{1,2,0:T(8,128)(2,1)S(1)} async-done(((bf16[8,1536,32]{1,2,0:T(8,128)(2,1)}), bf16[8,1536,32]{1,2,0:T(8,128)(2,1)S(1)}, u32[]{:S(2)}, u32[]{:S(2)}) %all-to-all-start.1) | async-done | bytes 786464 | tf_op jit(solution)/shard_map/all_to_all | solution.py:48
  25.5 0.1 copy.42
  25.6 77.3 %all-gather.5.cloned.1.call-done = bf16[128,12288]{0,1:T(8,128)(2,1)} async-done(((bf16[128,192]{0,1:T(8,128)(2,1)}), bf16[128,12288]{0,1:T(8,128)(2,1)}) %all-gather.5.cloned.1.call-update) | async-done | bytes 3145744 | tf_op jit(solution)/shard_map/all_gather | solution.py:52
  102.9 3.2 multiply_reduce_fusion
  106.2 0.0 copy-done.1
  106.2 0.6 fusion.17
  106.8 0.7 copy.35
  107.5 7.1 %all-to-all-start.2 = ((bf16[64,2,32]{2,1,0:T(2,128)(2,1)}), bf16[64,2,32]{2,1,0:T(2,128)(2,1)S(1)}, u32[]{:S(2)}, u32[]{:S(2)}) async-start(bf16[64,2,32]{2,1,0:T(2,128)(2,1)} %bitcast.1), calls=%async_computation.2 | async-start | bytes 65536 | tf_op jit(solution)/shard_map/all_to_all | solution.py:62
  114.6 1.9 gather_fusion
  116.5 1.8 copy.43
  118.3 3.3 gather_fusion.1
  121.6 3.1 copy.44
  124.7 1.6 all-to-all-done.2
  126.3 0.1 all_to_all.50
  126.4 0.0 copy-start.2
  126.4 38.2 %all-gather.7.cloned.1.call-done = bf16[12288,192]{0,1:T(8,128)(2,1)} async-done(((bf16[1536,192]{0,1:T(8,128)(2,1)}), bf16[12288,192]{0,1:T(8,128)(2,1)}) %all-gather.7.cloned.1.call-update) | async-done | bytes 4718608 | tf_op jit(solution)/shard_map/all_gather | solution.py:46
  164.6 4.7 %fusion.16 = bf16[128,192]{0,1:T(8,128)(2,1)S(1)} fusion(bf16[12288,192]{0,1:T(8,128)(2,1)} %all-gather.7.cloned.1.call-done, bf16[128,12288]{0,1:T(8,128)(2,1)} %all-gather.5.cloned.1.call-done, f32[128]{0:T(128)S(1)} %add_rsqrt_fusion), kind=kOutput, calls=%fused_computation.12 | convolution fusion | flops 604028928 | bytes 7913984 | tf_op jit(solution)/shard_map/dot_general | solution.py:54
  169.4 0.1 copy.31
  169.5 0.7 all_to_all.43
  170.1 12.4 %all-to-all-start = ((bf16[64,2,192]{2,1,0:T(2,128)(2,1)}), bf16[64,2,192]{2,1,0:T(2,128)(2,1)S(1)}, u32[]{:S(2)}, u32[]{:S(2)}) async-start(bf16[64,2,192]{2,1,0:T(2,128)(2,1)} %all_to_all.43), calls=%async_computation | async-start | bytes 131072 | tf_op jit(solution)/shard_map/all_to_all | solution.py:61
  182.6 0.0 all-gather.9.cloned.1.call-start
  182.7 13.0 %all-to-all-done = bf16[64,2,192]{2,1,0:T(2,128)(2,1)S(1)} async-done(((bf16[64,2,192]{2,1,0:T(2,128)(2,1)}), bf16[64,2,192]{2,1,0:T(2,128)(2,1)S(1)}, u32[]{:S(2)}, u32[]{:S(2)}) %all-to-all-start) | async-done | bytes 49184 | tf_op jit(solution)/shard_map/all_to_all | solution.py:61
  195.6 0.1 reshape.68
  195.8 0.1 fusion.24
  195.9 0.7 fusion.23
  196.7 0.2 fusion.18
  196.9 1.9 fusion.13
  198.8 0.1 all_to_all.51
  198.9 0.1 copy.38
  199.0 16.9 %all_to_all.59 = bf16[2,64,192]{2,0,1:T(2,128)(2,1)S(1)} all-to-all(bf16[2,64,192]{2,0,1:T(2,128)(2,1)S(1)} %copy.38), channel_id=1, replica_groups=mesh['group'=8,'tp'=64] {'tp'}, dimensions={1} | all-to-all | bytes 98304 | tf_op jit(solution)/shard_map/all_to_all | solution.py:65
  215.9 0.1 all_to_all.54
  215.9 0.7 copy.39
  216.7 0.0 all-gather.9.cloned.1.call-update
  216.7 13.9 %all-gather.11.cloned.1.call-done = bf16[12288,192]{0,1:T(8,128)(2,1)} async-done(((bf16[1536,192]{0,1:T(8,128)(2,1)}), bf16[12288,192]{0,1:T(8,128)(2,1)}) %all-gather.11.cloned.1.call-update) | async-done | bytes 4718608 | tf_op jit(solution)/shard_map/all_gather | solution.py:51
  230.6 88.0 %all-gather.9.cloned.1.call-done = bf16[128,12288]{0,1:T(8,128)(2,1)} async-done(((bf16[128,192]{0,1:T(8,128)(2,1)}), bf16[128,12288]{0,1:T(8,128)(2,1)}) %all-gather.9.cloned.1.call-update) | async-done | bytes 3145744 | tf_op jit(solution)/shard_map/all_gather | solution.py:67
  318.5 5.3 %convolution_convert_fusion = bf16[128,192]{0,1:T(8,128)(2,1)} fusion(bf16[12288,192]{0,1:T(8,128)(2,1)} %all-gather.11.cloned.1.call-done, bf16[128,12288]{0,1:T(8,128)(2,1)} %all-gather.9.cloned.1.call-done), kind=kOutput, calls=%fused_computation.13 | convolution fusion | flops 604004352 | bytes 7913472 | tf_op jit(solution)/shard_map/dot_general | solution.py:66
  (16 shorter events, 0.1 us)
Async XLA Ops:
  7.2 107.4 %copy-start = (bf16[24,32,1024]{2,1,0:T(8,128)(2,1)S(1)}, bf16[24,32,1024]{2,1,0:T(8,128)(2,1)}, u32[]{:S(2)}) copy-start(bf16[24,32,1024]{2,1,0:T(8,128)(2,1)} %param.12) | copy-start | bytes 4718596
  7.2 10.0 %copy-start.3 = (s32[2,12]{1,0:T(2,128)S(1)}, s32[2,12]{1,0:T(2,128)}, u32[]{:S(2)}) copy-start(s32[2,12]{1,0:T(2,128)} %param.14) | copy-start | bytes 292
  7.2 10.1 %copy-start.4 = (s32[2]{0:T(128)S(1)}, s32[2]{0:T(128)}, u32[]{:S(2)}) copy-start(s32[2]{0:T(128)} %param.15) | copy-start | bytes 28
  7.2 95.7 %all-gather.5.cloned.1.call-start = ((), (), s32[]{:S(2)}) async-start(), calls=%async_computation.4 | async-start | bytes 3194880 | tf_op jit(solution)/shard_map/all_gather | solution.py:52
  7.9 156.7 %all-gather.7.cloned.1.call-start = ((), (), s32[]{:S(2)}) async-start(), calls=%async_computation.5 | async-start | bytes 5308416 | tf_op jit(solution)/shard_map/all_gather | solution.py:46
  8.7 221.9 %all-gather.11.cloned.1.call-start = ((), (), s32[]{:S(2)}) async-start(), calls=%async_computation.7 | async-start | bytes 5308416 | tf_op jit(solution)/shard_map/all_gather | solution.py:51
  11.3 14.2 %all-to-all-start.1 = ((bf16[8,1536,32]{1,2,0:T(8,128)(2,1)}), bf16[8,1536,32]{1,2,0:T(8,128)(2,1)S(1)}, u32[]{:S(2)}, u32[]{:S(2)}) async-start(bf16[8,1536,32]{1,2,0:T(8,128)(2,1)} %stack.2), calls=%async_computation.1 | async-start | bytes 1572864 | tf_op jit(solution)/shard_map/all_to_all | solution.py:48
  102.9 3.2 copy-start.1
  107.5 18.8 %all-to-all-start.2 = ((bf16[64,2,32]{2,1,0:T(2,128)(2,1)}), bf16[64,2,32]{2,1,0:T(2,128)(2,1)S(1)}, u32[]{:S(2)}, u32[]{:S(2)}) async-start(bf16[64,2,32]{2,1,0:T(2,128)(2,1)} %bitcast.1), calls=%async_computation.2 | async-start | bytes 65536 | tf_op jit(solution)/shard_map/all_to_all | solution.py:62
  126.4 56.2 %copy-start.2 = (bf16[2,2048]{1,0:T(2,128)(2,1)}, bf16[2,2048]{1,0:T(2,128)(2,1)S(1)}, u32[]{:S(2)}) copy-start(bf16[2,2048]{1,0:T(2,128)(2,1)S(1)} %all_to_all.50) | copy-start | bytes 24580
  170.1 25.5 %all-to-all-start = ((bf16[64,2,192]{2,1,0:T(2,128)(2,1)}), bf16[64,2,192]{2,1,0:T(2,128)(2,1)S(1)}, u32[]{:S(2)}, u32[]{:S(2)}) async-start(bf16[64,2,192]{2,1,0:T(2,128)(2,1)} %all_to_all.43), calls=%async_computation | async-start | bytes 131072 | tf_op jit(solution)/shard_map/all_to_all | solution.py:61
  182.6 135.9 %all-gather.9.cloned.1.call-start = ((), (), s32[]{:S(2)}) async-start(), calls=%async_computation.6 | async-start | bytes 3194880 | tf_op jit(solution)/shard_map/all_gather | solution.py:67
Sparse Core Ops, SparseCore 0:
  11.4 91.5 all-gather.4
  105.0 59.5 all-gather.6
  166.7 63.7 all-gather.10
  234.3 84.1 all-gather.8
